TPU v7x, 512 devices: a whole 4x8x8 slice. The times are simulated.
512 devices in a mesh: dp: 32 (over y, z_lo, core), shard: 16 (over x, z_hi).
Axes of the slice: x: 4, y: 8, z: 8 (z_hi: 4, z_lo: 2; z = z_hi * 2 + z_lo), core: 2. Of those that a mesh axis runs over, the one named last changes fastest.
Arguments:
- queries: bfloat16 [65536, 2048], P(('dp', 'shard')), may hold values from -6 to 6
- keys_in: bfloat16 [65536, 2048], P(('dp', 'shard')), may hold values from -6 to 6
- values: bfloat16 [65536, 2048], P(('dp', 'shard')), may hold values from -6 to 6
- out_grad: bfloat16 [65536, 2048], P(('dp', 'shard')), may hold values from -48 to 48
- out_weight: bfloat16 [2048, 2048], P('shard'), may hold values from -0.125 to 0.125
- block_lists: int32 [32, 16, 4], P('dp'), may hold values from 0 to 15, as said below
- voxel_count: int32 [32], P('dp'), may hold values from 1024 to 2048
Outputs:
- grad_query: bfloat16 [65536, 2048], P(('dp', 'shard'))
- grad_key: bfloat16 [65536, 2048], P(('dp', 'shard'))
- grad_value: bfloat16 [65536, 2048], P(('dp', 'shard'))
- grad_weight: bfloat16 [2048, 2048], P('shard')
Inputs may be any that keep to these rules, and one draw needn't show every extreme that they name: `block_lists`: entry 0 of row b of a scene's list is b itself; the 4 entries of a row are different blocks of that scene.
All inputs are finite; a program needn't handle non-finite values.
Results may differ from a plain program's by a relative error of at most 0.0095.
Values may be sent and summed in bfloat16 or wider, within the bound.
A program may use at most 128 MiB of HBM per device.

v0:
```python
import math

import jax
import jax.numpy as jnp
from jax import lax
from jax.sharding import PartitionSpec as P

HDIM = 128
BLOCK = 128
NB = 4


def attend(queries, keys_in, values, block_ids, live_count):
    row_count, width_all = queries.shape
    head_count = width_all // HDIM
    block_count = row_count // BLOCK
    score_scale = 1.0 / math.sqrt(HDIM)
    query_blk = queries.reshape(block_count, BLOCK, head_count, HDIM)
    key_blk = keys_in.reshape(block_count, BLOCK, head_count, HDIM)[block_ids].reshape(
        block_count, NB * BLOCK, head_count, HDIM
    )
    value_blk = values.reshape(block_count, BLOCK, head_count, HDIM)[block_ids].reshape(
        block_count, NB * BLOCK, head_count, HDIM
    )
    query_pos = jnp.arange(row_count, dtype=jnp.int32).reshape(block_count, BLOCK)
    key_pos = (
        block_ids[:, :, None] * BLOCK + jnp.arange(BLOCK, dtype=jnp.int32)[None, None, :]
    ).reshape(block_count, NB * BLOCK)
    allowed = (key_pos[:, None, :] < live_count) | (query_pos[:, :, None] >= live_count)
    scores = (
        jnp.einsum("bqhd,bkhd->bhqk", query_blk, key_blk, preferred_element_type=jnp.float32)
        * score_scale
    )
    scores = jnp.where(allowed[:, None], scores, -jnp.inf)
    peak = jnp.max(scores, axis=-1, keepdims=True)
    weights = jnp.exp(scores - peak)
    probs = weights / jnp.sum(weights, axis=-1, keepdims=True)
    return (query_blk, key_blk, value_blk, probs)


def body(queries, keys_in, values, out_grad, out_weight, block_lists, voxel_count):
    local_rows = queries.shape[0]
    live_count = voxel_count[0]
    block_ids = block_lists[0]
    positions = lax.axis_index("shard") * local_rows + jnp.arange(local_rows, dtype=jnp.int32)
    grad_live = jnp.where((positions < live_count)[:, None], out_grad, jnp.zeros_like(out_grad))
    query_head, key_head, value_head = (
        lax.all_to_all(queries, "shard", split_axis=1, concat_axis=0, tiled=True),
        lax.all_to_all(keys_in, "shard", split_axis=1, concat_axis=0, tiled=True),
        lax.all_to_all(values, "shard", split_axis=1, concat_axis=0, tiled=True),
    )
    row_count, width_all = query_head.shape
    head_count = width_all // HDIM
    block_count = row_count // BLOCK
    score_scale = 1.0 / math.sqrt(HDIM)
    query_blk, key_blk, value_blk, probs = attend(
        query_head, key_head, value_head, block_ids, live_count
    )
    prob_bf = probs.astype(jnp.bfloat16)
    heads_out = (
        jnp.einsum("bhqk,bkhd->bqhd", prob_bf, value_blk, preferred_element_type=jnp.float32)
        .reshape(row_count, width_all)
        .astype(jnp.bfloat16)
    )
    row_piece = lax.all_gather(grad_live, "shard", axis=0, tiled=True)
    acc_now = jnp.einsum("rw,ro->wo", heads_out, row_piece, preferred_element_type=jnp.float32)
    product = jnp.einsum("ro,wo->rw", row_piece, out_weight, preferred_element_type=jnp.float32)
    grad_o = product.astype(jnp.bfloat16).reshape(block_count, BLOCK, head_count, HDIM)
    grad_prob = jnp.einsum("bqhd,bkhd->bhqk", grad_o, value_blk, preferred_element_type=jnp.float32)
    row_delta = jnp.sum(probs * grad_prob, axis=-1, keepdims=True)
    dscore = (probs * (grad_prob - row_delta) * score_scale).astype(jnp.bfloat16)
    grad_query = (
        jnp.einsum("bhqk,bkhd->bqhd", dscore, key_blk, preferred_element_type=jnp.float32)
        .reshape(row_count, width_all)
        .astype(jnp.bfloat16)
    )
    onehot = (
        block_ids[:, :, None] == jnp.arange(block_count, dtype=jnp.int32)[None, None, :]
    ).astype(jnp.float32)
    key_parts = jnp.einsum(
        "bhqk,bqhd->bkhd", dscore, query_blk, preferred_element_type=jnp.float32
    ).reshape(block_count, NB, BLOCK, width_all)
    value_parts = jnp.einsum(
        "bhqk,bqhd->bkhd", prob_bf, grad_o, preferred_element_type=jnp.float32
    ).reshape(block_count, NB, BLOCK, width_all)
    grad_key = (
        jnp.einsum("bjc,bjrx->crx", onehot, key_parts, precision=lax.Precision.HIGHEST)
        .reshape(row_count, width_all)
        .astype(jnp.bfloat16)
    )
    grad_value = (
        jnp.einsum("bjc,bjrx->crx", onehot, value_parts, precision=lax.Precision.HIGHEST)
        .reshape(row_count, width_all)
        .astype(jnp.bfloat16)
    )
    query_back, key_back, value_back = (
        lax.all_to_all(grad_query, "shard", split_axis=0, concat_axis=1, tiled=True),
        lax.all_to_all(grad_key, "shard", split_axis=0, concat_axis=1, tiled=True),
        lax.all_to_all(grad_value, "shard", split_axis=0, concat_axis=1, tiled=True),
    )
    scene_total = lax.axis_size("dp")
    summed = lax.psum(acc_now, "dp")
    grad_weight = (summed / scene_total).astype(jnp.bfloat16)
    return (query_back, key_back, value_back, grad_weight)


def solution(mesh):
    return jax.shard_map(
        body,
        mesh=mesh,
        in_specs=(
            P(("dp", "shard"), None),
            P(("dp", "shard"), None),
            P(("dp", "shard"), None),
            P(("dp", "shard"), None),
            P("shard", None),
            P("dp", None, None),
            P("dp"),
        ),
        out_specs=(
            P(("dp", "shard"), None),
            P(("dp", "shard"), None),
            P(("dp", "shard"), None),
            P("shard", None),
        ),
        check_vma=False,
    )
```

profile of v0, /device:TPU:1, one launch (start us, length us, event | category | flops | bytes accessed | tf_op | source)
XLA Modules:
  0.0 480.4 jit_solution(16984926543442195582)
XLA Ops:
  12.3 13.4 %all-to-all-start = ((bf16[128,16,128]{2,0,1:T(8,128)(2,1)}), bf16[128,16,128]{2,0,1:T(8,128)(2,1)S(1)}, u32[]{:S(2)}, u32[]{:S(2)}) async-start(bf16[128,16,128]{2,0,1:T(8,128)(2,1)} %copy.77), calls=%async_computation | async-start | bytes 1048576 | tf_op jit(solution)/shard_map/all_to_all | solution.py:49
  27.0 14.0 %all-to-all-done = bf16[128,16,128]{2,0,1:T(8,128)(2,1)S(1)} async-done(((bf16[128,16,128]{2,0,1:T(8,128)(2,1)}), bf16[128,16,128]{2,0,1:T(8,128)(2,1)S(1)}, u32[]{:S(2)}, u32[]{:S(2)}) %all-to-all-start) | async-done | bytes 524320 | tf_op jit(solution)/shard_map/all_to_all | solution.py:49
  41.1 4.3 all-to-all-start.2
  46.7 26.5 %all-to-all-done.2 = bf16[128,16,128]{2,0,1:T(8,128)(2,1)S(1)} async-done(((bf16[128,16,128]{2,0,1:T(8,128)(2,1)}), bf16[128,16,128]{2,0,1:T(8,128)(2,1)S(1)}, u32[]{:S(2)}, u32[]{:S(2)}) %all-to-all-start.2) | async-done | bytes 524320 | tf_op jit(solution)/shard_map/all_to_all | solution.py:50
  73.2 4.5 all-to-all-start.1
  82.4 31.9 %all-to-all-done.1 = bf16[128,16,128]{2,0,1:T(8,128)(2,1)S(1)} async-done(((bf16[128,16,128]{2,0,1:T(8,128)(2,1)}), bf16[128,16,128]{2,0,1:T(8,128)(2,1)S(1)}, u32[]{:S(2)}, u32[]{:S(2)}) %all-to-all-start.1) | async-done | bytes 524320 | tf_op jit(solution)/shard_map/all_to_all | solution.py:48
  116.7 5.0 %fusion.50 = (f32[16,128]{1,0:T(8,128)S(1)}, f32[16,128,512]{1,2,0:T(8,128)}) fusion(f32[16,512,128]{2,1,0:T(8,128)S(1)} %fusion.36, pred[16,128]{1,0:T(8,128)(4,1)S(1)} %add_compare_fusion, pred[16,512]{1,0:T(8,128)(4,1)S(1)} %fusion.38), kind=kOutput, calls=%fused_computation.55 | output fusion | flops 8389119 | bytes 8407040 | tf_op jit(solution)/shard_map/sub | solution.py:36
  121.8 37.5 %all-gather.2.cloned.1.call-done = bf16[2048,2048]{1,0:T(8,128)(2,1)} async-done(((bf16[128,2048]{1,0:T(8,128)(2,1)}), bf16[2048,2048]{1,0:T(8,128)(2,1)}) %all-gather.2.cloned.1.call-update) | async-done | bytes 8388624 | tf_op jit(solution)/shard_map/all_gather | solution.py:65
  159.3 5.7 %convolution_convert_fusion = bf16[2048,128]{1,0:T(8,128)(2,1)S(1)} fusion(bf16[2048,2048]{1,0:T(8,128)(2,1)} %all-gather.2.cloned.1.call-done, bf16[128,2048]{1,0:T(8,128)(2,1)S(1)} %copy-done), kind=kOutput, calls=%fused_computation.14 | convolution fusion | flops 1074003968 | bytes 9437184 | tf_op jit(solution)/shard_map/ro,wo->rw/dot_general | solution.py:67
  167.7 9.1 %fusion.9 = f32[16,512,128]{2,1,0:T(8,128)} fusion(f32[16,128,512]{1,2,0:T(8,128)} %fusion.51, bf16[128,16,128]{2,0,1:T(8,128)(2,1)S(1)} %all-to-all-done.1, f32[16,128,512]{1,2,0:T(8,128)} %get-tuple-element.25, f32[16,128]{1,0:T(8,128)S(1)} %get-tuple-element.24), kind=kOutput, calls=%fused_computation.12 | convolution fusion | flops 275778048 | bytes 13115392 | tf_op jit(solution)/shard_map/bhqk,bqhd->bkhd/dot_general | solution.py:80
  176.8 6.6 %fusion.24 = bf16[16,128,128]{2,0,1:T(8,128)(2,1)S(1)} fusion(f32[16,4,128,128]{3,2,1,0:T(8,128)} %bitcast.107, s32[16,4]{0,1:T(4,128)S(1)} %bitcast.118), kind=kOutput, calls=%fused_computation.26 | convolution fusion | flops 201589760 | bytes 4718848 | tf_op jit(solution)/shard_map/bjc,bjrx->crx/dot_general | solution.py:87
  184.3 8.4 %all-to-all-start.4 = ((bf16[16,128,128]{2,1,0:T(8,128)(2,1)}), bf16[16,128,128]{2,1,0:T(8,128)(2,1)S(1)}, u32[]{:S(2)}, u32[]{:S(2)}) async-start(bf16[16,128,128]{2,1,0:T(8,128)(2,1)} %copy.89), calls=%async_computation.4 | async-start | bytes 1048576 | tf_op jit(solution)/shard_map/all_to_all | solution.py:98
  192.7 4.5 convolution_convert_fusion.1
  197.2 8.6 %fusion.30 = bf16[16,128,128]{1,2,0:T(8,128)(2,1)} fusion(bf16[16,512,128]{2,1,0:T(8,128)(2,1)S(1)} %bitcast.104, f32[16,128,512]{1,2,0:T(8,128)} %fusion.51, f32[16,128,512]{1,2,0:T(8,128)} %get-tuple-element.25, f32[16,128]{1,0:T(8,128)S(1)} %get-tuple-element.24), kind=kOutput, calls=%fused_computation.29 | convolution fusion | flops 276040192 | bytes 11018240 | tf_op jit(solution)/shard_map/bhqk,bkhd->bqhd/dot_general | solution.py:73
  205.8 4.3 all-to-all-done.4
  210.1 4.8 all-to-all-start.3
  214.9 5.0 %convolution_bitcast_fusion = f32[16,512,1,128]{1,3,0,2:T(8,128)} fusion(bf16[16,128,128]{2,1,0:T(8,128)(2,1)} %bitcast.116, f32[16,128,512]{1,2,0:T(8,128)} %get-tuple-element.25, f32[16,128]{1,0:T(8,128)S(1)} %get-tuple-element.24), kind=kOutput, calls=%fused_computation.15 | convolution fusion | flops 270532608 | bytes 8921088 | tf_op jit(solution)/shard_map/bhqk,bqhd->bkhd/dot_general | solution.py:83
  220.0 5.3 %reshape.198 = f32[16,4,128,128]{2,1,3,0:T(4,128)} reshape(f32[16,512,1,128]{1,3,0,2:T(8,128)} %convolution_bitcast_fusion) | data formatting | bytes 8388608 | tf_op jit(solution)/shard_map/reshape | solution.py:85
  225.2 6.0 %copy.93 = f32[16,4,128,128]{3,0,1,2:T(8,128)} copy(f32[16,4,128,128]{2,1,3,0:T(4,128)} %reshape.198) | data formatting | bytes 8388608 | tf_op jit(solution)/shard_map/reshape | solution.py:85
  231.2 5.7 %fusion.52 = f32[128,2048]{1,0:T(8,128)} fusion(bf16[2048,128]{1,0:T(8,128)(2,1)S(1)} %bitcast.114, bf16[2048,2048]{1,0:T(8,128)(2,1)} %all-gather.2.cloned.1.call-done), kind=kOutput, calls=%fused_computation.57 | convolution fusion | flops 1073741824 | bytes 9961472 | tf_op jit(solution)/shard_map/rw,ro->wo/dot_general | solution.py:66
  237.0 4.3 fusion.23
  242.2 9.1 %all-to-all-start.5 = ((bf16[16,128,128]{2,1,0:T(8,128)(2,1)}), bf16[16,128,128]{2,1,0:T(8,128)(2,1)S(1)}, u32[]{:S(2)}, u32[]{:S(2)}) async-start(bf16[16,128,128]{2,1,0:T(8,128)(2,1)} %copy.94), calls=%async_computation.5 | async-start | bytes 1048576 | tf_op jit(solution)/shard_map/all_to_all | solution.py:99
  253.6 15.9 %all-to-all-done.5 = bf16[16,128,128]{2,1,0:T(8,128)(2,1)S(1)} async-done(((bf16[16,128,128]{2,1,0:T(8,128)(2,1)}), bf16[16,128,128]{2,1,0:T(8,128)(2,1)S(1)}, u32[]{:S(2)}, u32[]{:S(2)}) %all-to-all-start.5) | async-done | bytes 524320 | tf_op jit(solution)/shard_map/all_to_all | solution.py:99
  270.8 200.6 %all-reduce.2.cloned.1.call-done = f32[128,2048]{1,0:T(8,128)} async-done(((f32[128,2048]{1,0:T(8,128)}), f32[128,2048]{1,0:T(8,128)}) %all-reduce.2.cloned.1.call-update) | async-done | bytes 1048592 | tf_op jit(solution)/shard_map/psum | solution.py:102
  (51 shorter events, 24.2 us)
Async XLA Ops:
  7.2 152.1 %copy-start = (bf16[128,2048]{1,0:T(8,128)(2,1)S(1)}, bf16[128,2048]{1,0:T(8,128)(2,1)}, u32[]{:S(2)}) copy-start(bf16[128,2048]{1,0:T(8,128)(2,1)} %param.11) | copy-start | bytes 1572868
  7.2 18.6 %copy-start.4 = (bf16[128,2048]{1,0:T(8,128)(2,1)S(1)}, bf16[128,2048]{1,0:T(8,128)(2,1)}, u32[]{:S(2)}) copy-start(bf16[128,2048]{1,0:T(8,128)(2,1)} %param.9) | copy-start | bytes 1572868
  7.2 38.2 %copy-start.5 = (bf16[128,2048]{1,0:T(8,128)(2,1)S(1)}, bf16[128,2048]{1,0:T(8,128)(2,1)}, u32[]{:S(2)}) copy-start(bf16[128,2048]{1,0:T(8,128)(2,1)} %param.7) | copy-start | bytes 1572868
  7.2 152.1 %all-gather.2.cloned.1.call-start = ((), (), s32[]{:S(2)}) async-start(), calls=%async_computation.6 | async-start | bytes 8912896 | tf_op jit(solution)/shard_map/all_gather | solution.py:65
  11.3 66.4 %copy-start.7 = (s32[1,16,4]{1,2,0:T(4,128)S(1)}, s32[1,16,4]{1,2,0:T(4,128)}, u32[]{:S(2)}) copy-start(s32[1,16,4]{1,2,0:T(4,128)} %param.12) | copy-start | bytes 772
  12.3 28.8 %all-to-all-start = ((bf16[128,16,128]{2,0,1:T(8,128)(2,1)}), bf16[128,16,128]{2,0,1:T(8,128)(2,1)S(1)}, u32[]{:S(2)}, u32[]{:S(2)}) async-start(bf16[128,16,128]{2,0,1:T(8,128)(2,1)} %copy.77), calls=%async_computation | async-start | bytes 1048576 | tf_op jit(solution)/shard_map/all_to_all | solution.py:49
  41.1 32.1 %all-to-all-start.2 = ((bf16[128,16,128]{2,0,1:T(8,128)(2,1)}), bf16[128,16,128]{2,0,1:T(8,128)(2,1)S(1)}, u32[]{:S(2)}, u32[]{:S(2)}) async-start(bf16[128,16,128]{2,0,1:T(8,128)(2,1)} %copy.83), calls=%async_computation.2 | async-start | bytes 1048576 | tf_op jit(solution)/shard_map/all_to_all | solution.py:50
  73.2 41.1 %all-to-all-start.1 = ((bf16[128,16,128]{2,0,1:T(8,128)(2,1)}), bf16[128,16,128]{2,0,1:T(8,128)(2,1)S(1)}, u32[]{:S(2)}, u32[]{:S(2)}) async-start(bf16[128,16,128]{2,0,1:T(8,128)(2,1)} %copy.81), calls=%async_computation.1 | async-start | bytes 1048576 | tf_op jit(solution)/shard_map/all_to_all | solution.py:48
  121.8 43.3 %copy-start.2 = (bf16[64,128,128]{2,1,0:T(8,128)(2,1)S(1)}, bf16[64,128,128]{2,1,0:T(8,128)(2,1)}, u32[]{:S(2)}) copy-start(bf16[64,128,128]{2,1,0:T(8,128)(2,1)} %gather_fusion.1) | copy-start | bytes 6291460
  165.0 2.7 copy-start.6
  184.3 25.8 %all-to-all-start.4 = ((bf16[16,128,128]{2,1,0:T(8,128)(2,1)}), bf16[16,128,128]{2,1,0:T(8,128)(2,1)S(1)}, u32[]{:S(2)}, u32[]{:S(2)}) async-start(bf16[16,128,128]{2,1,0:T(8,128)(2,1)} %copy.89), calls=%async_computation.4 | async-start | bytes 1048576 | tf_op jit(solution)/shard_map/all_to_all | solution.py:98
  192.7 4.6 copy-start.1
  210.1 32.1 %all-to-all-start.3 = ((bf16[16,128,128]{1,2,0:T(8,128)(2,1)}), bf16[16,128,128]{1,2,0:T(8,128)(2,1)S(1)}, u32[]{:S(2)}, u32[]{:S(2)}) async-start(bf16[16,128,128]{1,2,0:T(8,128)(2,1)} %fusion.30), calls=%async_computation.3 | async-start | bytes 1048576 | tf_op jit(solution)/shard_map/all_to_all | solution.py:97
  214.9 256.6 %all-reduce.2.cloned.1.call-start = ((), (), s32[]{:S(2)}) async-start(), calls=%async_computation.7 | async-start | bytes 2097152 | tf_op jit(solution)/shard_map/psum | solution.py:102
  225.2 6.0 %copy-start.3 = (bf16[16,128,128]{1,2,0:T(8,128)(2,1)S(1)}, bf16[16,128,128]{1,2,0:T(8,128)(2,1)}, u32[]{:S(2)}) copy-start(bf16[16,128,128]{1,2,0:T(8,128)(2,1)} %convolution_convert_fusion.1) | copy-start | bytes 1572868
  242.2 27.3 %all-to-all-start.5 = ((bf16[16,128,128]{2,1,0:T(8,128)(2,1)}), bf16[16,128,128]{2,1,0:T(8,128)(2,1)S(1)}, u32[]{:S(2)}, u32[]{:S(2)}) async-start(bf16[16,128,128]{2,1,0:T(8,128)(2,1)} %copy.94), calls=%async_computation.5 | async-start | bytes 1048576 | tf_op jit(solution)/shard_map/all_to_all | solution.py:99
Sparse Core Ops, SparseCore 0:
  11.6 147.6 all-gather.1
  237.1 234.3 all-reduce.1
where the time goes:
time: 482 us; the launch traced here: 480 us
  waiting for transfers between devices  331 us (69%)
  matrix products  54.7 us (11%)
  starting transfers between devices  44.4 us (9%)
  local copies, waits for them, and re-layouts  26.3 us (5%)
  between operations  15 us (3%)
  other arithmetic  9.11 us (2%)
    psum x1, waiting for transfers between devices, body(): summed = lax.psum(acc_now, 'dp')  201 us
    all_gather x1, waiting for transfers between devices, body(): row_piece = lax.all_gather(grad_live, 'shard', axis=0, tiled=True)  37.5 us
    all_to_all x1, waiting for transfers between devices, body(): lax.all_to_all(queries, 'shard', split_axis=1, concat_axis=0, tiled=True)  31.9 us
    all_to_all x1, waiting for transfers between devices, body(): lax.all_to_all(values, 'shard', split_axis=1, concat_axis=0, tiled=True)  26.5 us
    all_to_all x1, waiting for transfers between devices, body(): lax.all_to_all(grad_value, 'shard', split_axis=0, concat_axis=1, tiled=True)  15.9 us
    all_to_all x1, waiting for transfers between devices, body(): lax.all_to_all(keys_in, 'shard', split_axis=1, concat_axis=0, tiled=True)  14 us
    all_to_all x1, starting transfers between devices, body(): lax.all_to_all(keys_in, 'shard', split_axis=1, concat_axis=0, tiled=True)  13.4 us
    reshape x2, local copies, waits for them, and re-layouts, body(): value_parts = jnp.einsum('bhqk,bqhd->bkhd', prob_bf, grad_o, preferred_el...  11.3 us
  transfers between devices with their start and end apart: 8, of which 7 were waited for; matrix products, arithmetic and copies ran while one was open for 13% of the time, Pallas kernels for 0%

commit v1 on v0

v1 whole, which is shorter than its diff:
```python
import math

import jax
import jax.numpy as jnp
from jax import lax
from jax.experimental import pallas as pl
from jax.experimental.pallas import tpu as pltpu
from jax.sharding import PartitionSpec as P

HDIM = 128
BLOCK = 128
NB = 4
NBLK = 16
WIDTH = 2048
HALF = BLOCK // 2
SCALE = 1.0 / math.sqrt(HDIM)
LOG2E = math.log2(math.e)
F32 = jnp.float32
BF16 = jnp.bfloat16
MESH = pl.DeviceIdType.MESH

NT = (((1,), (1,)), ((), ()))
NN = (((1,), (0,)), ((), ()))


def dot(a, b, dims):
    return lax.dot_general(a, b, dims, preferred_element_type=F32)


def order(i):
    return i + i // 2 - 2 * (i // 3)


def kernel(
    parts,
    q_in, k_in, v_in, g_in, w_ref, lists, count,
    dq_out, dk_out, dv_out, dw_out,
    qh, kh, vh, kt, vt, gall, probs, heads, dqb, kpart, vpart, kacc, vacc, dkb, dvb,
    wacc, wbf, wrecv, wres,
    qkv_recv, g_recv, out_recv, w_recv, send_sem, local_sem,
):
    me = lax.axis_index("shard")
    scene = lax.axis_index("dp")
    row_parts, col_parts = parts
    scenes = row_parts * col_parts
    wrow, wcol = BLOCK // row_parts, WIDTH // col_parts
    x, z = me // 4, me % 4
    x_up, x_down = ((x + 1) % 4) * 4 + z, ((x + 3) % 4) * 4 + z
    z_up, z_down = x * 4 + (z + 1) % 4, x * 4 + (z + 3) % 4
    live = count[0]

    def columns(index):
        return pl.ds(pl.multiple_of(index * HDIM, HDIM), HDIM)

    barrier = pltpu.get_barrier_semaphore()

    @pl.loop(1, NBLK)
    def _(o):
        pl.semaphore_signal(barrier, inc=1, device_id={"shard": (me + o) % NBLK}, device_id_type=MESH)

    @pl.loop(1, scenes)
    def _(o):
        pl.semaphore_signal(barrier, inc=1, device_id={"dp": (scene + o) % scenes}, device_id_type=MESH)

    pl.semaphore_wait(barrier, NBLK - 1 + scenes - 1)

    def push(src, dst, send, recv, shard):
        pltpu.make_async_remote_copy(
            src_ref=src, dst_ref=dst, send_sem=send, recv_sem=recv,
            device_id={"shard": shard}, device_id_type=MESH,
        ).start()

    def await_bytes(ref, sem):
        pltpu.make_async_copy(ref, ref, sem).wait()

    def block_at(dx, dz):
        return ((x + dx) % 4) * 4 + (z + dz) % 4

    def g_ref(dx, dz, half):
        ref = gall.at[block_at(dx, dz)]
        return ref if half is None else ref.at[pl.ds(half * HALF, HALF)]

    def g_push(src, dx, dz, half, target, rdx, rdz):
        push(src, g_ref(dx, dz, half), send_sem.at[0],
             g_recv.at[rdx * 4 + rdz, 0 if half is None else half], target)

    def g_wait(dx, dz, half):
        await_bytes(g_ref(dx, dz, half), g_recv.at[dx * 4 + dz, 0 if half is None else half])

    def g_along_x(src, dz, half):
        g_push(src, 0, dz, half, x_up, 3, dz)
        g_push(src, 0, dz, half, x_down, 1, dz)

    g_push(g_in, 0, 0, None, z_up, 0, 3)
    g_push(g_in, 0, 0, None, z_down, 0, 1)
    g_along_x(g_in, 0, None)
    for i, (src, dst) in enumerate(((q_in, qh), (k_in, kh), (v_in, vh))):
        @pl.loop(1, NBLK)
        def _(o, i=i, src=src, dst=dst):
            peer = (me + o) % NBLK
            push(src.at[:, columns(peer)], dst.at[me], send_sem.at[1], qkv_recv.at[i], peer)

    own = [
        pltpu.make_async_copy(g_in, gall.at[me], local_sem.at[0]),
        pltpu.make_async_copy(q_in.at[:, columns(me)], qh.at[me], local_sem.at[1]),
        pltpu.make_async_copy(k_in.at[:, columns(me)], kh.at[me], local_sem.at[2]),
        pltpu.make_async_copy(v_in.at[:, columns(me)], vh.at[me], local_sem.at[3]),
    ]
    for copy in own:
        copy.start()
    kacc[...] = jnp.zeros_like(kacc)
    vacc[...] = jnp.zeros_like(vacc)
    for copy in own:
        copy.wait()

    def forward_x(dz, first, second):
        g_wait(3, dz, first)
        g_push(g_ref(3, dz, 0), 3, dz, 0, x_up, 2, dz)
        g_wait(1, dz, second)
        g_push(g_ref(1, dz, 1), 1, dz, 1, x_down, 2, dz)

    forward_x(0, None, None)
    g_wait(0, 3, None)
    g_push(g_ref(0, 3, 0), 0, 3, 0, z_up, 0, 2)
    g_along_x(g_ref(0, 3, None), 3, None)
    g_wait(0, 1, None)
    g_push(g_ref(0, 1, 1), 0, 1, 1, z_down, 0, 2)
    g_along_x(g_ref(0, 1, None), 1, None)
    for half in range(2):
        g_wait(0, 2, half)
        g_along_x(g_ref(0, 2, half), 2, half)
    forward_x(3, None, None)
    forward_x(1, None, None)

    for i, dst in enumerate((qh, kh, vh)):
        await_bytes(dst.at[pl.ds(0, NBLK - 1)], qkv_recv.at[i])

    @pl.loop(0, NBLK)
    def _(b):
        kt[b] = kh[b].T
        vt[b] = vh[b].T

    lane = lax.broadcasted_iota(jnp.int32, (BLOCK, BLOCK), 1)
    sublane = lax.broadcasted_iota(jnp.int32, (BLOCK, BLOCK), 0)

    @pl.loop(0, NBLK)
    def _(b):
        ids = [lists[0, b, j] for j in range(NB)]
        keys = jnp.concatenate([kh[c] for c in ids], axis=0)
        scores = dot(keys, qh[b], NT) * (SCALE * LOG2E)
        query_pos = b * BLOCK + lane
        dead_query = query_pos >= live
        allowed = jnp.concatenate([((c * BLOCK + sublane) < live) | dead_query for c in ids], axis=0)
        scores = jnp.where(allowed, scores, -jnp.inf)
        peak = jnp.max(scores, axis=0, keepdims=True)
        weights = jnp.exp2(scores - peak)
        prob = weights * (1.0 / jnp.sum(weights, axis=0, keepdims=True))
        probs[b] = prob
        values_t = jnp.concatenate([vt[c] for c in ids], axis=1)
        head_t = dot(values_t, prob.astype(BF16), NN)
        heads[:, columns(b)] = jnp.where(dead_query, 0.0, head_t).astype(BF16)

    forward_x(2, 0, 1)
    g_wait(3, 2, 1)
    g_wait(1, 2, 0)

    def backward(b):
        ids = [lists[0, b, j] for j in range(NB)]
        dead_query = (b * BLOCK + lane) >= live
        da_t = jnp.where(dead_query, 0.0, dot(w_ref[...], gall[b], NT)).astype(BF16)
        prob = probs[b]
        grad_prob = dot(jnp.concatenate([vh[c] for c in ids], axis=0), da_t, NN)
        delta = jnp.sum(prob * grad_prob, axis=0, keepdims=True)
        dscore = (prob * (grad_prob - delta) * SCALE).astype(BF16)
        keys_t = jnp.concatenate([kt[c] for c in ids], axis=1)
        dqb[b] = dot(keys_t, dscore, NN).T.astype(BF16)
        kpart[...] = dot(dscore, qh[b], NN).reshape(NB, BLOCK, HDIM)
        vpart[...] = dot(prob.astype(BF16), da_t, NT).reshape(NB, BLOCK, HDIM)
        for c in range(NBLK):
            place, gain = 0, 0.0
            for j in range(NB):
                place = jnp.where(ids[j] == c, j, place)
                gain = jnp.where(ids[j] == c, 1.0, gain)
            kacc[c] += gain * kpart[place]
            vacc[c] += gain * vpart[place]

    def send_dq(b):
        push(dqb.at[b], dq_out.at[:, columns(me)], send_sem.at[1], out_recv.at[0], b)

    @pl.loop(0, 12)
    def _(t):
        b = block_at(order(t % 3), order(t // 3))
        backward(b)

        @pl.when(t > 0)
        def _():
            send_dq(b)

    @pl.loop(0, 4)
    def _(t):
        dz = order(t)
        b = block_at(2, dz)
        await_bytes(gall.at[b, pl.ds(0, HALF)], g_recv.at[8 + dz, 0])
        await_bytes(gall.at[b, pl.ds(HALF, HALF)], g_recv.at[8 + dz, 1])
        backward(b)
        send_dq(b)

    dkb[...] = kacc[...].astype(BF16)
    dvb[...] = vacc[...].astype(BF16)

    @pl.loop(1, NBLK)
    def _(o):
        peer = (me + o) % NBLK
        push(dkb.at[peer], dk_out.at[:, columns(me)], send_sem.at[1], out_recv.at[1], peer)
        push(dvb.at[peer], dv_out.at[:, columns(me)], send_sem.at[1], out_recv.at[2], peer)

    back = [
        pltpu.make_async_copy(src.at[me], dst.at[:, columns(me)], local_sem.at[i])
        for i, (src, dst) in enumerate(((dqb, dq_out), (dkb, dk_out), (dvb, dv_out)))
    ]
    for copy in back:
        copy.start()

    tile = 256

    @pl.loop(0, WIDTH // tile)
    def _(t):
        at = pl.ds(pl.multiple_of(t * tile, tile), tile)
        out = dot(heads[...], gall[:, :, at].reshape(NBLK * BLOCK, tile), NN)
        wacc[:, at] = out
        wbf[:, at] = out.astype(BF16)

    def piece(index):
        return (
            pl.ds(pl.multiple_of((index // col_parts) * wrow, wrow), wrow),
            pl.ds(pl.multiple_of((index % col_parts) * wcol, wcol), wcol),
        )

    def push_dp(src, dst, send, recv, peer):
        pltpu.make_async_remote_copy(
            src_ref=src, dst_ref=dst, send_sem=send, recv_sem=recv,
            device_id={"dp": peer}, device_id_type=MESH,
        ).start()

    @pl.loop(1, scenes)
    def _(o):
        peer = (scene + o) % scenes
        push_dp(wbf.at[piece(peer)], wrecv.at[o - 1], send_sem.at[2], w_recv.at[0], peer)

    await_bytes(wrecv, w_recv.at[0])
    total = wacc[piece(scene)]
    for i in range(scenes - 1):
        total = total + wrecv[i].astype(F32)
    wres[...] = (total * (1.0 / scenes)).astype(BF16)

    @pl.loop(1, scenes)
    def _(o):
        peer = (scene + o) % scenes
        push_dp(wres, dw_out.at[piece(scene)], send_sem.at[3], w_recv.at[1], peer)

    keep = pltpu.make_async_copy(wres, dw_out.at[piece(scene)], local_sem.at[3])
    keep.start()
    keep.wait()
    for copy in back:
        copy.wait()
    await_bytes(wrecv, w_recv.at[1])
    for i, out in enumerate((dq_out, dk_out, dv_out)):
        await_bytes(out.at[:, pl.ds(0, WIDTH - HDIM)], out_recv.at[i])
    await_bytes(gall.at[pl.ds(0, NBLK - 1)], send_sem.at[0])
    for dst in (qh, kh, vh, dqb, dkb, dvb):
        await_bytes(dst.at[pl.ds(0, NBLK - 1)], send_sem.at[1])
    await_bytes(wrecv, send_sem.at[2])
    await_bytes(wrecv, send_sem.at[3])


def body(queries, keys_in, values, out_grad, out_weight, block_lists, voxel_count):
    scenes = lax.axis_size("dp")
    row_parts = min(8, scenes)
    col_parts = scenes // row_parts
    wrow, wcol = BLOCK // row_parts, WIDTH // col_parts
    blocks = (NBLK, BLOCK, HDIM)
    hbm = pl.BlockSpec(memory_space=pl.ANY)
    vmem = pl.BlockSpec(memory_space=pltpu.VMEM)
    smem = pl.BlockSpec(memory_space=pltpu.SMEM)
    rows = jax.ShapeDtypeStruct((BLOCK, WIDTH), BF16)

    def run(*refs):
        kernel((row_parts, col_parts), *refs)

    return pl.pallas_call(
        run,
        out_shape=(rows, rows, rows, rows),
        in_specs=[hbm, hbm, hbm, hbm, vmem, smem, smem],
        out_specs=(hbm, hbm, hbm, hbm),
        scratch_shapes=[
            pltpu.VMEM(blocks, BF16),
            pltpu.VMEM(blocks, BF16),
            pltpu.VMEM(blocks, BF16),
            pltpu.VMEM(blocks, BF16),
            pltpu.VMEM(blocks, BF16),
            pltpu.VMEM((NBLK, BLOCK, WIDTH), BF16),
            pltpu.VMEM((NBLK, NB * BLOCK, BLOCK), F32),
            pltpu.VMEM((HDIM, NBLK * BLOCK), BF16),
            pltpu.VMEM(blocks, BF16),
            pltpu.VMEM((NB, BLOCK, HDIM), F32),
            pltpu.VMEM((NB, BLOCK, HDIM), F32),
            pltpu.VMEM(blocks, F32),
            pltpu.VMEM(blocks, F32),
            pltpu.VMEM(blocks, BF16),
            pltpu.VMEM(blocks, BF16),
            pltpu.VMEM((BLOCK, WIDTH), F32),
            pltpu.VMEM((BLOCK, WIDTH), BF16),
            pltpu.VMEM((scenes - 1, wrow, wcol), BF16),
            pltpu.VMEM((wrow, wcol), BF16),
            pltpu.SemaphoreType.DMA((3,)),
            pltpu.SemaphoreType.DMA((16, 2)),
            pltpu.SemaphoreType.DMA((3,)),
            pltpu.SemaphoreType.DMA((2,)),
            pltpu.SemaphoreType.DMA((4,)),
            pltpu.SemaphoreType.DMA((4,)),
        ],
        compiler_params=pltpu.CompilerParams(
            collective_id=0, has_side_effects=True, vmem_limit_bytes=48 * 1024 * 1024
        ),
        cost_estimate=pl.CostEstimate(flops=4_000_000_000, bytes_accessed=8_000_000, transcendentals=1_000_000),
    )(queries, keys_in, values, out_grad, out_weight, block_lists, voxel_count)


def solution(mesh):
    return jax.shard_map(
        body,
        mesh=mesh,
        in_specs=(
            P(("dp", "shard"), None),
            P(("dp", "shard"), None),
            P(("dp", "shard"), None),
            P(("dp", "shard"), None),
            P("shard", None),
            P("dp", None, None),
            P("dp"),
        ),
        out_specs=(
            P(("dp", "shard"), None),
            P(("dp", "shard"), None),
            P(("dp", "shard"), None),
            P("shard", None),
        ),
        check_vma=False,
    )
```

time: 482 us -> 185 us (0.38)
  waiting for transfers between devices: 331 us -> 0 us
  Pallas kernels: 0 us -> 174 us
  matrix products: 54.7 us -> 0 us
  starting transfers between devices: 44.4 us -> 0 us
  local copies, waits for them, and re-layouts: 26.3 us -> 9.14 us
  between operations: 15 us -> 1.29 us
  other arithmetic: 9.11 us -> 0 us
    psum x1 -> x0, waiting for transfers between devices: 201 us -> none  [body(): summed = lax.psum(acc_now, 'dp')]
    pallas_call x0 -> x1, Pallas kernels: none -> 174 us  [body(): pl.pallas_call(run, out_shape=(rows, rows, rows, rows), in_specs=[hbm, hb...]
    all_to_all x6 -> x0, waiting for transfers between devices: 92.7 us -> none  [the longest x1 31.9 us: body(): lax.all_to_all(queries, 'shard', split_axis=1, concat_axis=0, tiled=True)]
    dot_general x10 -> x0, matrix products: 54.7 us -> none  [the longest x1 9.14 us: body(): jnp.einsum('bhqk,bqhd->bkhd', dscore, query_blk, preferred_element_type=j...]
    all_to_all x6 -> x0, starting transfers between devices: 44.4 us -> none  [the longest x1 13.4 us: body(): lax.all_to_all(keys_in, 'shard', split_axis=1, concat_axis=0, tiled=True)]
    all_gather x1 -> x0, waiting for transfers between devices: 37.5 us -> none  [body(): row_piece = lax.all_gather(grad_live, 'shard', axis=0, tiled=True)]
    reshape x2 -> x0, local copies, waits for them, and re-layouts: 11.3 us -> none  [body(): value_parts = jnp.einsum('bhqk,bqhd->bkhd', prob_bf, grad_o, preferred_el...]
    sub x1 -> x0, other arithmetic: 5.04 us -> none  [attend(): weights = jnp.exp(scores - peak)]
  transfers between devices with their start and end apart: 8 -> 0, of which waited for: 7 -> 0; matrix products, arithmetic and copies ran while one was open for 13% -> 0% of each run, Pallas kernels for 0% -> 0%
where the time goes in v1:
time: 185 us
  Pallas kernels  174 us (94%)
  local copies, waits for them, and re-layouts  9.14 us (5%)
    pallas_call x1, Pallas kernels, body(): pl.pallas_call(run, out_shape=(rows, rows, rows, rows), in_specs=[hbm, hb...  174 us
    unnamed x15, local copies, waits for them, and re-layouts  9.14 us

profile of v1, /device:TPU:1, one launch (start us, length us, event | category | flops | bytes accessed | tf_op | source)
XLA Modules:
  0.0 184.9 jit_solution(11812842686273821064)
XLA Ops:
  1.3 0.8 copy.11.refs_5_
  2.0 0.0 copy-start
  2.0 1.0 copy-done
  3.1 0.0 copy-start.1
  3.1 1.0 copy-done.1
  4.1 0.0 copy-start.2
  4.1 1.0 copy-done.2
  5.2 0.0 copy-start.3
  5.2 1.0 copy-done.3
  6.2 0.0 copy-start.4
  6.2 1.0 copy-done.4
  7.2 174.5 %shard_map.102 = (bf16[128,2048]{1,0:T(8,128)(2,1)S(1)}, bf16[128,2048]{1,0:T(8,128)(2,1)S(1)}, bf16[128,2048]{1,0:T(8,128)(2,1)S(1)}, bf16[128,2048]{1,0:T(8,128)(2,1)S(1)}) custom-call(bf16[128,2048]{1,0:T(8,128)(2,1)S(1)} %copy-done, bf16[128,2048]{1,0:T(8,128)(2,1)S(1)} %copy-done.1, bf16[128,2048]{1,0:T(8,128)(2,1)S(1)} %copy-done.2, ...), custom_call_target="tpu_custom_call" | custom-call | flops 4000000000 | bytes 8000000 | tf_op jit(solution)/shard_map/pallas_call | solution.py:290
  181.7 0.8 copy.17
  182.5 0.8 copy.18
  183.3 0.8 copy.19
  184.1 0.8 copy.20
Async XLA Ops:
  2.0 1.0 copy-start
  3.1 1.0 copy-start.1
  4.1 1.0 copy-start.2
  5.2 1.0 copy-start.3
  6.2 1.0 copy-start.4

commit v2 on v1

v2 whole, which is shorter than its diff:
```python
import math

import jax
import jax.numpy as jnp
from jax import lax
from jax.experimental import pallas as pl
from jax.experimental.pallas import tpu as pltpu
from jax.sharding import PartitionSpec as P

HDIM = 128
BLOCK = 128
NB = 4
NBLK = 16
WIDTH = 2048
HALF = BLOCK // 2
QUART = BLOCK // 4
SCALE = 1.0 / math.sqrt(HDIM)
LOG2E = math.log2(math.e)
F32 = jnp.float32
BF16 = jnp.bfloat16
MESH = pl.DeviceIdType.MESH

NT = (((1,), (1,)), ((), ()))
NN = (((1,), (0,)), ((), ()))


def dot(a, b, dims):
    return lax.dot_general(a, b, dims, preferred_element_type=F32)


def order(i):
    return i + i // 2 - 2 * (i // 3)


def kernel(
    parts,
    q_in, k_in, v_in, g_in, w_in, lists, count,
    dq_out, dk_out, dv_out, dw_out,
    qh, kh, vh, kt, vt, gall, probs, heads, dqb, kpart, vpart, kacc, vacc, dkb, dvb,
    w_ref, wacc, wbf, wcore, whalf, whbf, wquart, wqbf, wrecv, wres,
    qkv_recv, g_recv, out_recv, w_recv, send_sem, local_sem,
):
    me = lax.axis_index("shard")
    scene = lax.axis_index("dp")
    row_parts, col_parts = parts
    rows_y = row_parts * col_parts
    scenes = 4 * rows_y
    wrow, wcol = QUART // row_parts, WIDTH // col_parts
    core, low, y = scene % 2, (scene // 2) % 2, scene // 4
    x, z = me // 4, me % 4
    x_up, x_down = ((x + 1) % 4) * 4 + z, ((x + 3) % 4) * 4 + z
    z_up, z_down = x * 4 + (z + 1) % 4, x * 4 + (z + 3) % 4
    live = count[0]

    def columns(index):
        return pl.ds(pl.multiple_of(index * HDIM, HDIM), HDIM)

    own = [
        pltpu.make_async_copy(g_in, gall.at[me], local_sem.at[0]),
        pltpu.make_async_copy(q_in.at[:, columns(me)], qh.at[me], local_sem.at[1]),
        pltpu.make_async_copy(k_in.at[:, columns(me)], kh.at[me], local_sem.at[2]),
        pltpu.make_async_copy(v_in.at[:, columns(me)], vh.at[me], local_sem.at[3]),
        pltpu.make_async_copy(w_in, w_ref, local_sem.at[4]),
    ]
    for copy in own:
        copy.start()

    barrier = pltpu.get_barrier_semaphore()

    @pl.loop(1, NBLK)
    def _(o):
        pl.semaphore_signal(barrier, inc=1, device_id={"shard": (me + o) % NBLK}, device_id_type=MESH)

    @pl.loop(1, rows_y)
    def _(o):
        pl.semaphore_signal(
            barrier, inc=1, device_id={"dp": ((y + o) % rows_y) * 4 + scene % 4}, device_id_type=MESH
        )

    other_core = scene + 1 - 2 * core
    other_low = scene + 2 - 4 * low
    for peer in (other_core, other_low):
        pl.semaphore_signal(barrier, inc=1, device_id={"dp": peer}, device_id_type=MESH)
    pl.semaphore_wait(barrier, NBLK - 1 + rows_y - 1 + 2)

    def push(src, dst, send, recv, shard):
        pltpu.make_async_remote_copy(
            src_ref=src, dst_ref=dst, send_sem=send, recv_sem=recv,
            device_id={"shard": shard}, device_id_type=MESH,
        ).start()

    def push_dp(src, dst, send, recv, peer):
        pltpu.make_async_remote_copy(
            src_ref=src, dst_ref=dst, send_sem=send, recv_sem=recv,
            device_id={"dp": peer}, device_id_type=MESH,
        ).start()

    def await_bytes(ref, sem):
        pltpu.make_async_copy(ref, ref, sem).wait()

    def block_at(dx, dz):
        return ((x + dx) % 4) * 4 + (z + dz) % 4

    def g_ref(dx, dz, half):
        return gall.at[block_at(dx, dz), pl.ds(half * HALF, HALF)]

    def g_push(dx, dz, half, target, rdx, rdz):
        src = g_in.at[pl.ds(half * HALF, HALF)] if (dx, dz) == (0, 0) else g_ref(dx, dz, half)
        push(src, g_ref(dx, dz, half), send_sem.at[0], g_recv.at[rdx * 4 + rdz, half], target)

    def g_wait(dx, dz, half):
        await_bytes(g_ref(dx, dz, half), g_recv.at[dx * 4 + dz, half])

    def along_x(dz, half):
        g_push(0, dz, half, x_up, 3, dz)
        g_push(0, dz, half, x_down, 1, dz)

    def pass_up(dz):
        g_wait(3, dz, 0)
        g_push(3, dz, 0, x_up, 2, dz)

    def pass_down(dz):
        g_wait(1, dz, 1)
        g_push(1, dz, 1, x_down, 2, dz)

    g_push(0, 0, 0, z_up, 0, 3)
    g_push(0, 0, 1, z_down, 0, 1)
    g_push(0, 0, 0, x_up, 3, 0)
    g_push(0, 0, 1, x_down, 1, 0)
    g_push(0, 0, 1, x_up, 3, 0)
    g_push(0, 0, 0, x_down, 1, 0)
    kacc[...] = jnp.zeros_like(kacc)
    vacc[...] = jnp.zeros_like(vacc)
    wacc[...] = jnp.zeros_like(wacc)
    kpart[NBLK] = jnp.zeros_like(kpart[NBLK])
    vpart[NBLK] = jnp.zeros_like(vpart[NBLK])

    pass_up(0)
    pass_down(0)
    g_wait(0, 3, 0)
    g_push(0, 3, 0, z_up, 0, 2)
    along_x(3, 0)
    g_wait(0, 1, 1)
    g_push(0, 1, 1, z_down, 0, 2)
    along_x(1, 1)

    for i, (src, dst) in enumerate(((q_in, qh), (k_in, kh), (v_in, vh))):
        @pl.loop(1, NBLK)
        def _(o, i=i, src=src, dst=dst):
            peer = (me + o) % NBLK
            push(src.at[:, columns(peer)], dst.at[me], send_sem.at[1], qkv_recv.at[i], peer)

    for half in range(2):
        g_wait(0, 2, half)
        along_x(2, half)
    pass_up(3)
    pass_down(1)
    pass_up(2)
    pass_down(2)

    for i, dst in enumerate((qh, kh, vh)):
        await_bytes(dst.at[pl.ds(0, NBLK - 1)], qkv_recv.at[i])
    g_push(0, 0, 1, z_up, 0, 3)
    g_push(0, 0, 0, z_down, 0, 1)
    for copy in own:
        copy.wait()

    @pl.loop(0, NBLK)
    def _(b):
        kt[b] = kh[b].T
        vt[b] = vh[b].T

    lane = lax.broadcasted_iota(jnp.int32, (BLOCK, BLOCK), 1)
    sublane = lax.broadcasted_iota(jnp.int32, (BLOCK, BLOCK), 0)

    def forward(b):
        ids = [lists[0, b, j] for j in range(NB)]
        keys = jnp.concatenate([kh[c] for c in ids], axis=0)
        scores = dot(keys, qh[b], NT) * (SCALE * LOG2E)
        query_pos = b * BLOCK + lane
        dead_query = query_pos >= live
        allowed = jnp.concatenate([((c * BLOCK + sublane) < live) | dead_query for c in ids], axis=0)
        scores = jnp.where(allowed, scores, -jnp.inf)
        peak = jnp.max(scores, axis=0, keepdims=True)
        weights = jnp.exp2(scores - peak)
        prob = weights * (1.0 / jnp.sum(weights, axis=0, keepdims=True))
        probs[b] = prob
        values_t = jnp.concatenate([vt[c] for c in ids], axis=1)
        head_t = dot(values_t, prob.astype(BF16), NN)
        heads[b] = jnp.where(dead_query, 0.0, head_t).astype(BF16)

    pl.loop(0, NBLK // 2)(forward)
    g_wait(0, 3, 1)
    along_x(3, 1)
    g_wait(0, 1, 0)
    along_x(1, 0)
    pl.loop(NBLK // 2, NBLK)(forward)

    def backward(slot, b):
        ids = [lists[0, b, j] for j in range(NB)]
        dead_query = (b * BLOCK + lane) >= live
        da_t = jnp.where(dead_query, 0.0, dot(w_ref[...], gall[b], NT)).astype(BF16)
        prob = probs[b]
        grad_prob = dot(jnp.concatenate([vh[c] for c in ids], axis=0), da_t, NN)
        delta = jnp.sum(prob * grad_prob, axis=0, keepdims=True)
        dscore = (prob * (grad_prob - delta) * SCALE).astype(BF16)
        keys_t = jnp.concatenate([kt[c] for c in ids], axis=1)
        dqb[b] = dot(keys_t, dscore, NN).T.astype(BF16)
        at = pl.ds(slot * NB, NB)
        kpart[at] = dot(dscore, qh[b], NN).reshape(NB, BLOCK, HDIM)
        vpart[at] = dot(prob.astype(BF16), da_t, NT).reshape(NB, BLOCK, HDIM)

    def add_parts(blocks):
        ids = [[lists[0, b, j] for j in range(NB)] for b in blocks]

        @pl.loop(0, NBLK)
        def _(c):
            key, value = kacc[c], vacc[c]
            for slot in range(NB):
                place = NBLK
                for j in range(NB):
                    place = jnp.where(ids[slot][j] == c, slot * NB + j, place)
                key = key + kpart[place]
                value = value + vpart[place]
            kacc[c] = key
            vacc[c] = value

    tile = 256

    def add_weight(blocks):
        head = jnp.concatenate([heads[b] for b in blocks], axis=1)

        @pl.loop(0, WIDTH // tile)
        def _(t):
            at = pl.ds(pl.multiple_of(t * tile, tile), tile)
            grad = jnp.concatenate([gall[b, :, at] for b in blocks], axis=0)
            wacc[:, at] += dot(head, grad, NN)

    def send_dq(b):
        push(dqb.at[b], dq_out.at[:, columns(me)], send_sem.at[1], out_recv.at[0], b)

    for dz in (0, 2):
        g_wait(3, dz, 1)
        g_wait(1, dz, 0)
        g_wait(2, dz, 0)
        g_wait(2, dz, 1)

    @pl.loop(0, 2)
    def _(g):
        @pl.loop(0, 4)
        def _(i):
            b = block_at(i, 2 * g)
            backward(i, b)

            @pl.when(g + i > 0)
            def _():
                send_dq(b)

        blocks = [block_at(i, 2 * g) for i in range(4)]
        add_parts(blocks)
        add_weight(blocks)

    pass_down(3)
    pass_up(1)

    for dz in (3, 1):
        g_wait(3, dz, 1)
        g_wait(1, dz, 0)

    @pl.loop(0, 4)
    def _(i):
        b = block_at(3 * (i // 2), 3 - 2 * (i % 2))
        backward(i, b)
        send_dq(b)

    blocks = [block_at(dx, dz) for dx in (0, 3) for dz in (3, 1)]
    add_parts(blocks)
    near, far = [[block_at(dx, dz) for dz in (3, 1)] for dx in (1, 2)]

    @pl.loop(0, 2)
    def _(i):
        b = block_at(1, 3 - 2 * i)
        backward(i, b)
        send_dq(b)

    add_weight(blocks + near)
    for dz in (3, 1):
        g_wait(2, dz, 0)
        g_wait(2, dz, 1)
    add_weight(far)
    wbf[...] = wacc[...].astype(BF16)

    def rows_at(index, size):
        return pl.ds(pl.multiple_of(index * size, size), size)

    push_dp(wbf.at[rows_at(1 - core, HALF)], wcore, send_sem.at[2], w_recv.at[0], other_core)

    @pl.loop(2, 4)
    def _(i):
        b = block_at(2, 7 - 2 * i)
        backward(i, b)
        send_dq(b)

    await_bytes(wcore, w_recv.at[0])
    whalf[...] = wacc[rows_at(core, HALF)] + wcore[...].astype(F32)
    whbf[...] = whalf[...].astype(BF16)
    push_dp(whbf.at[rows_at(1 - low, QUART)], wquart, send_sem.at[3], w_recv.at[1], other_low)

    add_parts(near + far)
    dkb[...] = kacc[...].astype(BF16)
    dvb[...] = vacc[...].astype(BF16)

    @pl.loop(1, NBLK)
    def _(o):
        peer = (me + o) % NBLK
        push(dkb.at[peer], dk_out.at[:, columns(me)], send_sem.at[1], out_recv.at[1], peer)
        push(dvb.at[peer], dv_out.at[:, columns(me)], send_sem.at[1], out_recv.at[2], peer)

    back = [
        pltpu.make_async_copy(src.at[me], dst.at[:, columns(me)], local_sem.at[i])
        for i, (src, dst) in enumerate(((dqb, dq_out), (dkb, dk_out), (dvb, dv_out)))
    ]
    for copy in back:
        copy.start()

    await_bytes(wquart, w_recv.at[1])
    mine = whalf[rows_at(low, QUART)] + wquart[...].astype(F32)
    whalf[pl.ds(0, QUART)] = mine
    wqbf[...] = mine.astype(BF16)

    def piece(index, first=0):
        return (
            pl.ds(pl.multiple_of(first + (index // col_parts) * wrow, wrow), wrow),
            pl.ds(pl.multiple_of((index % col_parts) * wcol, wcol), wcol),
        )

    @pl.loop(1, rows_y)
    def _(o):
        peer = (y + o) % rows_y
        push_dp(wqbf.at[piece(peer)], wrecv.at[o - 1], send_sem.at[4], w_recv.at[2], peer * 4 + scene % 4)

    total = whalf[piece(y)]
    if rows_y > 1:
        await_bytes(wrecv, w_recv.at[2])
        for i in range(rows_y - 1):
            total = total + wrecv[i].astype(F32)
    wres[...] = (total * (1.0 / scenes)).astype(BF16)
    place = dw_out.at[piece(y, core * HALF + low * QUART)]

    @pl.loop(1, rows_y)
    def _(o):
        peer = (y + o) % rows_y
        push_dp(wres, place, send_sem.at[5], w_recv.at[3], peer * 4 + scene % 4)

    keep = pltpu.make_async_copy(wres, place, local_sem.at[3])
    keep.start()
    keep.wait()
    if rows_y > 1:
        await_bytes(wrecv, w_recv.at[3])
    quart = dw_out.at[rows_at(core * 2 + low, QUART)]
    push_dp(quart, quart, send_sem.at[6], w_recv.at[4], other_low)
    await_bytes(wquart, w_recv.at[4])
    half = dw_out.at[rows_at(core, HALF)]
    push_dp(half, half, send_sem.at[7], w_recv.at[5], other_core)

    for copy in back:
        copy.wait()
    for i, out in enumerate((dq_out, dk_out, dv_out)):
        await_bytes(out.at[:, pl.ds(0, WIDTH - HDIM)], out_recv.at[i])
    await_bytes(wcore, w_recv.at[5])
    await_bytes(gall.at[pl.ds(0, NBLK - 1)], send_sem.at[0])
    for dst in (qh, kh, vh, dqb, dkb, dvb):
        await_bytes(dst.at[pl.ds(0, NBLK - 1)], send_sem.at[1])
    await_bytes(wcore, send_sem.at[2])
    await_bytes(wquart, send_sem.at[3])
    if rows_y > 1:
        await_bytes(wrecv, send_sem.at[4])
        await_bytes(wrecv, send_sem.at[5])
    await_bytes(wquart, send_sem.at[6])
    await_bytes(wcore, send_sem.at[7])


def body(queries, keys_in, values, out_grad, out_weight, block_lists, voxel_count):
    scenes = lax.axis_size("dp")
    rows_y = scenes // 4
    row_parts = min(2, rows_y)
    col_parts = rows_y // row_parts
    wrow, wcol = QUART // row_parts, WIDTH // col_parts
    blocks = (NBLK, BLOCK, HDIM)
    hbm = pl.BlockSpec(memory_space=pl.ANY)
    smem = pl.BlockSpec(memory_space=pltpu.SMEM)
    rows = jax.ShapeDtypeStruct((BLOCK, WIDTH), BF16)

    def run(*refs):
        kernel((row_parts, col_parts), *refs)

    return pl.pallas_call(
        run,
        out_shape=(rows, rows, rows, rows),
        in_specs=[hbm, hbm, hbm, hbm, hbm, smem, smem],
        out_specs=(hbm, hbm, hbm, hbm),
        scratch_shapes=[
            pltpu.VMEM(blocks, BF16),
            pltpu.VMEM(blocks, BF16),
            pltpu.VMEM(blocks, BF16),
            pltpu.VMEM(blocks, BF16),
            pltpu.VMEM(blocks, BF16),
            pltpu.VMEM((NBLK, BLOCK, WIDTH), BF16),
            pltpu.VMEM((NBLK, NB * BLOCK, BLOCK), F32),
            pltpu.VMEM(blocks, BF16),
            pltpu.VMEM(blocks, BF16),
            pltpu.VMEM((NBLK + 1, BLOCK, HDIM), F32),
            pltpu.VMEM((NBLK + 1, BLOCK, HDIM), F32),
            pltpu.VMEM(blocks, F32),
            pltpu.VMEM(blocks, F32),
            pltpu.VMEM(blocks, BF16),
            pltpu.VMEM(blocks, BF16),
            pltpu.VMEM((BLOCK, WIDTH), BF16),
            pltpu.VMEM((BLOCK, WIDTH), F32),
            pltpu.VMEM((BLOCK, WIDTH), BF16),
            pltpu.VMEM((HALF, WIDTH), BF16),
            pltpu.VMEM((HALF, WIDTH), F32),
            pltpu.VMEM((HALF, WIDTH), BF16),
            pltpu.VMEM((QUART, WIDTH), BF16),
            pltpu.VMEM((QUART, WIDTH), BF16),
            pltpu.VMEM((max(rows_y - 1, 1), wrow, wcol), BF16),
            pltpu.VMEM((wrow, wcol), BF16),
            pltpu.SemaphoreType.DMA((3,)),
            pltpu.SemaphoreType.DMA((16, 2)),
            pltpu.SemaphoreType.DMA((3,)),
            pltpu.SemaphoreType.DMA((6,)),
            pltpu.SemaphoreType.DMA((8,)),
            pltpu.SemaphoreType.DMA((5,)),
        ],
        compiler_params=pltpu.CompilerParams(
            collective_id=0, has_side_effects=True, vmem_limit_bytes=60 * 1024 * 1024
        ),
        cost_estimate=pl.CostEstimate(flops=4_000_000_000, bytes_accessed=8_000_000, transcendentals=1_000_000),
    )(queries, keys_in, values, out_grad, out_weight, block_lists, voxel_count)


def solution(mesh):
    return jax.shard_map(
        body,
        mesh=mesh,
        in_specs=(
            P(("dp", "shard"), None),
            P(("dp", "shard"), None),
            P(("dp", "shard"), None),
            P(("dp", "shard"), None),
            P("shard", None),
            P("dp", None, None),
            P("dp"),
        ),
        out_specs=(
            P(("dp", "shard"), None),
            P(("dp", "shard"), None),
            P(("dp", "shard"), None),
            P("shard", None),
        ),
        check_vma=False,
    )
```

time: 185 us -> 160 us (0.86)
  Pallas kernels: 174 us -> 152 us
  local copies, waits for them, and re-layouts: 9.14 us -> 6.55 us
    pallas_call x1, Pallas kernels: 174 us -> 152 us  [body(): pl.pallas_call(run, out_shape=(rows, rows, rows, rows), in_specs=[hbm, hb...]
    unnamed x15 -> x11, local copies, waits for them, and re-layouts: 9.14 us -> 6.55 us
where the time goes in v2:
time: 160 us
  Pallas kernels  152 us (95%)
  local copies, waits for them, and re-layouts  6.55 us (4%)
    pallas_call x1, Pallas kernels, body(): pl.pallas_call(run, out_shape=(rows, rows, rows, rows), in_specs=[hbm, hb...  152 us
    unnamed x11, local copies, waits for them, and re-layouts  6.55 us

profile of v2, /device:TPU:1, one launch (start us, length us, event | category | flops | bytes accessed | tf_op | source)
XLA Modules:
  0.0 160.0 jit_solution(15554660219516573645)
XLA Ops:
  1.3 1.4 copy.11.refs_5_
  2.6 152.1 %shard_map.102 = (bf16[128,2048]{1,0:T(8,128)(2,1)}, bf16[128,2048]{1,0:T(8,128)(2,1)}, bf16[128,2048]{1,0:T(8,128)(2,1)}, bf16[128,2048]{1,0:T(8,128)(2,1)}) custom-call(bf16[128,2048]{1,0:T(8,128)(2,1)} %refs_0_.1, bf16[128,2048]{1,0:T(8,128)(2,1)} %refs_1_.1, bf16[128,2048]{1,0:T(8,128)(2,1)} %refs_2_.1, bf16[128,2048]{1,0:T(8,128)(2,1)} %refs_3_.1, ...), custom_call_target="tpu_custom_call" | custom-call | flops 4000000000 | bytes 8000000 | tf_op jit(solution)/shard_map/pallas_call | solution.py:397
  154.8 0.0 copy-start.2
  154.8 1.9 %copy.17 = bf16[128,2048]{1,0:T(8,128)(2,1)} copy(bf16[128,2048]{1,0:T(8,128)(2,1)} %get-tuple-element.8) | data formatting | bytes 1048576
  156.7 0.0 copy-done.2
  156.7 0.0 copy-start.1
  156.7 0.8 copy.18
  157.5 0.4 copy-done.1
  157.9 0.0 copy-start
  157.9 0.8 copy.19
  158.7 0.4 copy-done
  159.2 0.8 copy.20
Async XLA Ops:
  154.8 2.0 %copy-start.2 = (bf16[128,2048]{1,0:T(8,128)(2,1)S(1)}, bf16[128,2048]{1,0:T(8,128)(2,1)}, u32[]{:S(2)}) copy-start(bf16[128,2048]{1,0:T(8,128)(2,1)} %get-tuple-element.9) | copy-start | bytes 1572868
  156.7 1.2 copy-start.1
  157.9 1.2 copy-start

commit v3 on v2

--- a/solution.py
+++ b/solution.py
@@ -34,11 +34,11 @@
 
 def kernel(
     parts,
-    q_in, k_in, v_in, g_in, w_in, lists, count,
+    q_in, k_in, v_in, g_in, w_in, lists_in, count,
     dq_out, dk_out, dv_out, dw_out,
-    qh, kh, vh, kt, vt, gall, probs, heads, dqb, kpart, vpart, kacc, vacc, dkb, dvb,
+    qx, kx, vx, qh, kh, vh, kt, vt, gall, probs, heads, dqb, kpart, vpart, kacc, vacc, dkb, dvb,
     w_ref, wacc, wbf, wcore, whalf, whbf, wquart, wqbf, wrecv, wres,
-    qkv_recv, g_recv, out_recv, w_recv, send_sem, local_sem,
+    lists, x_recv, qkv_recv, g_recv, out_recv, w_recv, send_sem, local_sem,
 ):
     me = lax.axis_index("shard")
     scene = lax.axis_index("dp")
@@ -55,12 +55,16 @@
     def columns(index):
         return pl.ds(pl.multiple_of(index * HDIM, HDIM), HDIM)
 
+    def heads_of(index):
+        return pl.ds(pl.multiple_of(index * 4 * HDIM, 4 * HDIM), 4 * HDIM)
+
     own = [
         pltpu.make_async_copy(g_in, gall.at[me], local_sem.at[0]),
-        pltpu.make_async_copy(q_in.at[:, columns(me)], qh.at[me], local_sem.at[1]),
-        pltpu.make_async_copy(k_in.at[:, columns(me)], kh.at[me], local_sem.at[2]),
-        pltpu.make_async_copy(v_in.at[:, columns(me)], vh.at[me], local_sem.at[3]),
+        pltpu.make_async_copy(q_in.at[:, heads_of(x)], qx.at[x], local_sem.at[1]),
+        pltpu.make_async_copy(k_in.at[:, heads_of(x)], kx.at[x], local_sem.at[2]),
+        pltpu.make_async_copy(v_in.at[:, heads_of(x)], vx.at[x], local_sem.at[3]),
         pltpu.make_async_copy(w_in, w_ref, local_sem.at[4]),
+        pltpu.make_async_copy(lists_in, lists, local_sem.at[5]),
     ]
     for copy in own:
         copy.start()
@@ -122,6 +126,12 @@
     def pass_down(dz):
         g_wait(1, dz, 1)
         g_push(1, dz, 1, x_down, 2, dz)
+
+    arrays = ((q_in, qx, qh), (k_in, kx, kh), (v_in, vx, vh))
+    for i, (src, mid, dst) in enumerate(arrays):
+        for o in (1, 3, 2):
+            to_x = (x + o) % 4
+            push(src.at[:, heads_of(to_x)], mid.at[x], send_sem.at[8], x_recv.at[i], to_x * 4 + z)
 
     g_push(0, 0, 0, z_up, 0, 3)
     g_push(0, 0, 1, z_down, 0, 1)
@@ -134,22 +144,27 @@
     wacc[...] = jnp.zeros_like(wacc)
     kpart[NBLK] = jnp.zeros_like(kpart[NBLK])
     vpart[NBLK] = jnp.zeros_like(vpart[NBLK])
-
-    pass_up(0)
-    pass_down(0)
+    for copy in own:
+        copy.wait()
+
+    def along_z(i):
+        src, mid, dst = arrays[i]
+        await_bytes(mid.at[pl.ds(0, 3)], x_recv.at[i])
+        for o in (1, 3, 2):
+            to_z = (z + o) % 4
+            push(mid.at[:, :, columns(to_z)], dst.at[:, z], send_sem.at[8], qkv_recv.at[i], x * 4 + to_z)
+        pltpu.make_async_copy(mid.at[:, :, columns(z)], dst.at[:, z], local_sem.at[i]).start()
+
     g_wait(0, 3, 0)
     g_push(0, 3, 0, z_up, 0, 2)
     along_x(3, 0)
     g_wait(0, 1, 1)
     g_push(0, 1, 1, z_down, 0, 2)
     along_x(1, 1)
-
-    for i, (src, dst) in enumerate(((q_in, qh), (k_in, kh), (v_in, vh))):
-        @pl.loop(1, NBLK)
-        def _(o, i=i, src=src, dst=dst):
-            peer = (me + o) % NBLK
-            push(src.at[:, columns(peer)], dst.at[me], send_sem.at[1], qkv_recv.at[i], peer)
-
+    for i in range(3):
+        along_z(i)
+    pass_up(0)
+    pass_down(0)
     for half in range(2):
         g_wait(0, 2, half)
         along_x(2, half)
@@ -158,25 +173,24 @@
     pass_up(2)
     pass_down(2)
 
-    for i, dst in enumerate((qh, kh, vh)):
-        await_bytes(dst.at[pl.ds(0, NBLK - 1)], qkv_recv.at[i])
     g_push(0, 0, 1, z_up, 0, 3)
     g_push(0, 0, 0, z_down, 0, 1)
-    for copy in own:
-        copy.wait()
+    for i, (src, mid, dst) in enumerate(arrays):
+        await_bytes(dst.at[pl.ds(0, 3)], qkv_recv.at[i])
+        pltpu.make_async_copy(mid.at[:, :, columns(z)], dst.at[:, z], local_sem.at[i]).wait()
 
     @pl.loop(0, NBLK)
     def _(b):
-        kt[b] = kh[b].T
-        vt[b] = vh[b].T
+        kt[b] = kh[b // 4, b % 4].T
+        vt[b] = vh[b // 4, b % 4].T
 
     lane = lax.broadcasted_iota(jnp.int32, (BLOCK, BLOCK), 1)
     sublane = lax.broadcasted_iota(jnp.int32, (BLOCK, BLOCK), 0)
 
     def forward(b):
-        ids = [lists[0, b, j] for j in range(NB)]
-        keys = jnp.concatenate([kh[c] for c in ids], axis=0)
-        scores = dot(keys, qh[b], NT) * (SCALE * LOG2E)
+        ids = [lists[0, j, b] for j in range(NB)]
+        keys = jnp.concatenate([kh[c // 4, c % 4] for c in ids], axis=0)
+        scores = dot(keys, qh[b // 4, b % 4], NT) * (SCALE * LOG2E)
         query_pos = b * BLOCK + lane
         dead_query = query_pos >= live
         allowed = jnp.concatenate([((c * BLOCK + sublane) < live) | dead_query for c in ids], axis=0)
@@ -197,21 +211,21 @@
     pl.loop(NBLK // 2, NBLK)(forward)
 
     def backward(slot, b):
-        ids = [lists[0, b, j] for j in range(NB)]
+        ids = [lists[0, j, b] for j in range(NB)]
         dead_query = (b * BLOCK + lane) >= live
         da_t = jnp.where(dead_query, 0.0, dot(w_ref[...], gall[b], NT)).astype(BF16)
         prob = probs[b]
-        grad_prob = dot(jnp.concatenate([vh[c] for c in ids], axis=0), da_t, NN)
+        grad_prob = dot(jnp.concatenate([vh[c // 4, c % 4] for c in ids], axis=0), da_t, NN)
         delta = jnp.sum(prob * grad_prob, axis=0, keepdims=True)
         dscore = (prob * (grad_prob - delta) * SCALE).astype(BF16)
         keys_t = jnp.concatenate([kt[c] for c in ids], axis=1)
         dqb[b] = dot(keys_t, dscore, NN).T.astype(BF16)
         at = pl.ds(slot * NB, NB)
-        kpart[at] = dot(dscore, qh[b], NN).reshape(NB, BLOCK, HDIM)
+        kpart[at] = dot(dscore, qh[b // 4, b % 4], NN).reshape(NB, BLOCK, HDIM)
         vpart[at] = dot(prob.astype(BF16), da_t, NT).reshape(NB, BLOCK, HDIM)
 
     def add_parts(blocks):
-        ids = [[lists[0, b, j] for j in range(NB)] for b in blocks]
+        ids = [[lists[0, j, b] for j in range(NB)] for b in blocks]
 
         @pl.loop(0, NBLK)
         def _(c):
@@ -369,8 +383,10 @@
         await_bytes(out.at[:, pl.ds(0, WIDTH - HDIM)], out_recv.at[i])
     await_bytes(wcore, w_recv.at[5])
     await_bytes(gall.at[pl.ds(0, NBLK - 1)], send_sem.at[0])
-    for dst in (qh, kh, vh, dqb, dkb, dvb):
+    for dst in (dqb, dkb, dvb):
         await_bytes(dst.at[pl.ds(0, NBLK - 1)], send_sem.at[1])
+    for mid in (qx, kx, vx, qx, kx, vx):
+        await_bytes(mid.at[pl.ds(0, 3)], send_sem.at[8])
     await_bytes(wcore, send_sem.at[2])
     await_bytes(wquart, send_sem.at[3])
     if rows_y > 1:
@@ -394,15 +410,18 @@
     def run(*refs):
         kernel((row_parts, col_parts), *refs)
 
-    return pl.pallas_call(
+    grads = pl.pallas_call(
         run,
         out_shape=(rows, rows, rows, rows),
-        in_specs=[hbm, hbm, hbm, hbm, hbm, smem, smem],
+        in_specs=[hbm, hbm, hbm, hbm, hbm, hbm, smem],
         out_specs=(hbm, hbm, hbm, hbm),
         scratch_shapes=[
-            pltpu.VMEM(blocks, BF16),
-            pltpu.VMEM(blocks, BF16),
-            pltpu.VMEM(blocks, BF16),
+            pltpu.VMEM((4, BLOCK, 4 * HDIM), BF16),
+            pltpu.VMEM((4, BLOCK, 4 * HDIM), BF16),
+            pltpu.VMEM((4, BLOCK, 4 * HDIM), BF16),
+            pltpu.VMEM((4, 4, BLOCK, HDIM), BF16),
+            pltpu.VMEM((4, 4, BLOCK, HDIM), BF16),
+            pltpu.VMEM((4, 4, BLOCK, HDIM), BF16),
             pltpu.VMEM(blocks, BF16),
             pltpu.VMEM(blocks, BF16),
             pltpu.VMEM((NBLK, BLOCK, WIDTH), BF16),
@@ -425,18 +444,41 @@
             pltpu.VMEM((QUART, WIDTH), BF16),
             pltpu.VMEM((max(rows_y - 1, 1), wrow, wcol), BF16),
             pltpu.VMEM((wrow, wcol), BF16),
+            pltpu.SMEM((1, NB, NBLK), jnp.int32),
+            pltpu.SemaphoreType.DMA((3,)),
             pltpu.SemaphoreType.DMA((3,)),
             pltpu.SemaphoreType.DMA((16, 2)),
             pltpu.SemaphoreType.DMA((3,)),
             pltpu.SemaphoreType.DMA((6,)),
-            pltpu.SemaphoreType.DMA((8,)),
-            pltpu.SemaphoreType.DMA((5,)),
+            pltpu.SemaphoreType.DMA((9,)),
+            pltpu.SemaphoreType.DMA((6,)),
         ],
         compiler_params=pltpu.CompilerParams(
             collective_id=0, has_side_effects=True, vmem_limit_bytes=60 * 1024 * 1024
         ),
         cost_estimate=pl.CostEstimate(flops=4_000_000_000, bytes_accessed=8_000_000, transcendentals=1_000_000),
-    )(queries, keys_in, values, out_grad, out_weight, block_lists, voxel_count)
+    )(queries, keys_in, values, out_grad, out_weight, jnp.transpose(block_lists, (0, 2, 1)), voxel_count)
+
+    def hand_over(*refs):
+        ins, outs, held, sems = refs[:4], refs[4:8], refs[8], refs[9]
+        reads = [pltpu.make_async_copy(src, held.at[i], sems.at[0, i]) for i, src in enumerate(ins)]
+        writes = [pltpu.make_async_copy(held.at[i], dst, sems.at[1, i]) for i, dst in enumerate(outs)]
+        for copy in reads:
+            copy.start()
+        for read, write in zip(reads, writes):
+            read.wait()
+            write.start()
+        for copy in writes:
+            copy.wait()
+
+    return pl.pallas_call(
+        hand_over,
+        out_shape=(rows, rows, rows, rows),
+        in_specs=[hbm] * 4,
+        out_specs=(hbm,) * 4,
+        scratch_shapes=[pltpu.VMEM((4, BLOCK, WIDTH), BF16), pltpu.SemaphoreType.DMA((2, 4))],
+        compiler_params=pltpu.CompilerParams(vmem_limit_bytes=60 * 1024 * 1024),
+    )(*grads)
 
 
 def solution(mesh):

time: 160 us -> 150 us (0.938)
  local copies, waits for them, and re-layouts: 6.55 us -> 0 us
  Pallas kernels: 152 us -> 149 us
    unnamed x11 -> x0, local copies, waits for them, and re-layouts: 6.55 us -> none
    pallas_call x1, Pallas kernels: 152 us -> 146 us  [body(): pl.pallas_call(run, out_shape=(rows, rows, rows, rows), in_specs=[hbm, hb...]
    pallas_call x0 -> x1, Pallas kernels: none -> 2.42 us  [body(): pl.pallas_call(hand_over, out_shape=(rows, rows, rows, rows), in_specs=[h...]
where the time goes in v3:
time: 150 us
  Pallas kernels  149 us (99%)
    pallas_call x1, Pallas kernels, body(): pl.pallas_call(run, out_shape=(rows, rows, rows, rows), in_specs=[hbm, hb...  146 us

profile of v3, /device:TPU:1, one launch (start us, length us, event | category | flops | bytes accessed | tf_op | source)
XLA Modules:
  0.0 149.9 jit_solution(3104739214101600304)
XLA Ops:
  1.3 146.1 %shard_map.102 = (bf16[128,2048]{1,0:T(8,128)(2,1)}, bf16[128,2048]{1,0:T(8,128)(2,1)}, bf16[128,2048]{1,0:T(8,128)(2,1)}, bf16[128,2048]{1,0:T(8,128)(2,1)}) custom-call(bf16[128,2048]{1,0:T(8,128)(2,1)} %refs_0_.1, bf16[128,2048]{1,0:T(8,128)(2,1)} %refs_1_.1, bf16[128,2048]{1,0:T(8,128)(2,1)} %refs_2_.1, bf16[128,2048]{1,0:T(8,128)(2,1)} %refs_3_.1, ...), custom_call_target="tpu_custom_call" | custom-call | flops 4000000000 | bytes 8000000 | tf_op jit(solution)/shard_map/pallas_call | solution.py:413
  147.4 2.4 %shard_map.103 = (bf16[128,2048]{1,0:T(8,128)(2,1)}, bf16[128,2048]{1,0:T(8,128)(2,1)}, bf16[128,2048]{1,0:T(8,128)(2,1)}, bf16[128,2048]{1,0:T(8,128)(2,1)}) custom-call(bf16[128,2048]{1,0:T(8,128)(2,1)} %get-tuple-element.8.refs_0_, bf16[128,2048]{1,0:T(8,128)(2,1)} %get-tuple-element.9.refs_1_, bf16[128,2048]{1,0:T(8,128)(2,1)} %get-tuple-element.10.refs_2_, ...), custom_call_target="tpu_custom_call" | custom-call | tf_op jit(solution)/shard_map/pallas_call | solution.py:474

commit v4 on v3

--- a/solution.py
+++ b/solution.py
@@ -36,7 +36,7 @@
     parts,
     q_in, k_in, v_in, g_in, w_in, lists_in, count,
     dq_out, dk_out, dv_out, dw_out,
-    qx, kx, vx, qh, kh, vh, kt, vt, gall, probs, heads, dqb, kpart, vpart, kacc, vacc, dkb, dvb,
+    da, qx, kx, vx, qh, kh, vh, kt, vt, gall, probs, heads, dqb, kpart, vpart, kacc, vacc, dkb, dvb,
     w_ref, wacc, wbf, wcore, whalf, whbf, wquart, wqbf, wrecv, wres,
     lists, x_recv, qkv_recv, g_recv, out_recv, w_recv, send_sem, local_sem,
 ):
@@ -175,6 +175,23 @@
 
     g_push(0, 0, 1, z_up, 0, 3)
     g_push(0, 0, 0, z_down, 0, 1)
+    lane = lax.broadcasted_iota(jnp.int32, (BLOCK, BLOCK), 1)
+    sublane = lax.broadcasted_iota(jnp.int32, (BLOCK, BLOCK), 0)
+
+    def grad_attn(b):
+        dead_query = (b * BLOCK + lane) >= live
+        return jnp.where(dead_query, 0.0, dot(w_ref[...], gall[b], NT)).astype(BF16)
+
+    g_wait(3, 0, 1)
+    g_wait(1, 0, 0)
+    g_wait(2, 0, 0)
+    g_wait(2, 0, 1)
+
+    @pl.loop(0, 4)
+    def _(i):
+        b = block_at(i, 0)
+        da[b] = grad_attn(b)
+
     for i, (src, mid, dst) in enumerate(arrays):
         await_bytes(dst.at[pl.ds(0, 3)], qkv_recv.at[i])
         pltpu.make_async_copy(mid.at[:, :, columns(z)], dst.at[:, z], local_sem.at[i]).wait()
@@ -183,9 +200,6 @@
     def _(b):
         kt[b] = kh[b // 4, b % 4].T
         vt[b] = vh[b // 4, b % 4].T
-
-    lane = lax.broadcasted_iota(jnp.int32, (BLOCK, BLOCK), 1)
-    sublane = lax.broadcasted_iota(jnp.int32, (BLOCK, BLOCK), 0)
 
     def forward(b):
         ids = [lists[0, j, b] for j in range(NB)]
@@ -203,17 +217,16 @@
         head_t = dot(values_t, prob.astype(BF16), NN)
         heads[b] = jnp.where(dead_query, 0.0, head_t).astype(BF16)
 
-    pl.loop(0, NBLK // 2)(forward)
+    pl.loop(0, NBLK // 2, unroll=2)(forward)
     g_wait(0, 3, 1)
     along_x(3, 1)
     g_wait(0, 1, 0)
     along_x(1, 0)
-    pl.loop(NBLK // 2, NBLK)(forward)
-
-    def backward(slot, b):
+    pl.loop(NBLK // 2, NBLK, unroll=2)(forward)
+
+    def backward(slot, b, early=False):
         ids = [lists[0, j, b] for j in range(NB)]
-        dead_query = (b * BLOCK + lane) >= live
-        da_t = jnp.where(dead_query, 0.0, dot(w_ref[...], gall[b], NT)).astype(BF16)
+        da_t = da[b] if early else grad_attn(b)
         prob = probs[b]
         grad_prob = dot(jnp.concatenate([vh[c // 4, c % 4] for c in ids], axis=0), da_t, NN)
         delta = jnp.sum(prob * grad_prob, axis=0, keepdims=True)
@@ -253,24 +266,25 @@
     def send_dq(b):
         push(dqb.at[b], dq_out.at[:, columns(me)], send_sem.at[1], out_recv.at[0], b)
 
-    for dz in (0, 2):
+    for dz in (2,):
         g_wait(3, dz, 1)
         g_wait(1, dz, 0)
         g_wait(2, dz, 0)
         g_wait(2, dz, 1)
 
-    @pl.loop(0, 2)
-    def _(g):
-        @pl.loop(0, 4)
-        def _(i):
-            b = block_at(i, 2 * g)
-            backward(i, b)
-
-            @pl.when(g + i > 0)
+    for dz in (0, 2):
+        @pl.loop(0, 4, step=2)
+        def _(i, dz=dz):
+            for j in range(2):
+                backward(i + j, block_at(i + j, dz), early=dz == 0)
+
+            @pl.when(dz + i > 0)
             def _():
-                send_dq(b)
-
-        blocks = [block_at(i, 2 * g) for i in range(4)]
+                send_dq(block_at(i, dz))
+
+            send_dq(block_at(i + 1, dz))
+
+        blocks = [block_at(dx, dz) for dx in range(4)]
         add_parts(blocks)
         add_weight(blocks)
 
@@ -281,20 +295,21 @@
         g_wait(3, dz, 1)
         g_wait(1, dz, 0)
 
-    @pl.loop(0, 4)
+    @pl.loop(0, 2)
     def _(i):
-        b = block_at(3 * (i // 2), 3 - 2 * (i % 2))
-        backward(i, b)
-        send_dq(b)
+        pair = [block_at(3 * i, dz) for dz in (3, 1)]
+        for j in range(2):
+            backward(2 * i + j, pair[j])
+        for b in pair:
+            send_dq(b)
 
     blocks = [block_at(dx, dz) for dx in (0, 3) for dz in (3, 1)]
     add_parts(blocks)
     near, far = [[block_at(dx, dz) for dz in (3, 1)] for dx in (1, 2)]
 
-    @pl.loop(0, 2)
-    def _(i):
-        b = block_at(1, 3 - 2 * i)
-        backward(i, b)
+    for i in range(2):
+        backward(i, near[i])
+    for b in near:
         send_dq(b)
 
     add_weight(blocks + near)
@@ -309,10 +324,9 @@
 
     push_dp(wbf.at[rows_at(1 - core, HALF)], wcore, send_sem.at[2], w_recv.at[0], other_core)
 
-    @pl.loop(2, 4)
-    def _(i):
-        b = block_at(2, 7 - 2 * i)
-        backward(i, b)
+    for i in range(2):
+        backward(2 + i, far[i])
+    for b in far:
         send_dq(b)
 
     await_bytes(wcore, w_recv.at[0])
@@ -416,6 +430,7 @@
         in_specs=[hbm, hbm, hbm, hbm, hbm, hbm, smem],
         out_specs=(hbm, hbm, hbm, hbm),
         scratch_shapes=[
+            pltpu.VMEM(blocks, BF16),
             pltpu.VMEM((4, BLOCK, 4 * HDIM), BF16),
             pltpu.VMEM((4, BLOCK, 4 * HDIM), BF16),
             pltpu.VMEM((4, BLOCK, 4 * HDIM), BF16),

time: 150 us -> 147 us (0.980)
  Pallas kernels: 149 us -> 145 us
    pallas_call x1, Pallas kernels: 146 us -> 143 us  [body(): pl.pallas_call(run, out_shape=(rows, rows, rows, rows), in_specs=[hbm, hb...]
where the time goes in v4:
time: 147 us
  Pallas kernels  145 us (99%)
    pallas_call x1, Pallas kernels, body(): pl.pallas_call(run, out_shape=(rows, rows, rows, rows), in_specs=[hbm, hb...  143 us

profile of v4, /device:TPU:1, one launch (start us, length us, event | category | flops | bytes accessed | tf_op | source)
XLA Modules:
  0.0 146.7 jit_solution(11255032025628599977)
XLA Ops:
  1.3 143.0 %shard_map.102 = (bf16[128,2048]{1,0:T(8,128)(2,1)}, bf16[128,2048]{1,0:T(8,128)(2,1)}, bf16[128,2048]{1,0:T(8,128)(2,1)}, bf16[128,2048]{1,0:T(8,128)(2,1)}) custom-call(bf16[128,2048]{1,0:T(8,128)(2,1)} %refs_0_.1, bf16[128,2048]{1,0:T(8,128)(2,1)} %refs_1_.1, bf16[128,2048]{1,0:T(8,128)(2,1)} %refs_2_.1, bf16[128,2048]{1,0:T(8,128)(2,1)} %refs_3_.1, ...), custom_call_target="tpu_custom_call" | custom-call | flops 4000000000 | bytes 8000000 | tf_op jit(solution)/shard_map/pallas_call | solution.py:427
  144.3 2.4 %shard_map.103 = (bf16[128,2048]{1,0:T(8,128)(2,1)}, bf16[128,2048]{1,0:T(8,128)(2,1)}, bf16[128,2048]{1,0:T(8,128)(2,1)}, bf16[128,2048]{1,0:T(8,128)(2,1)}) custom-call(bf16[128,2048]{1,0:T(8,128)(2,1)} %get-tuple-element.8.refs_0_, bf16[128,2048]{1,0:T(8,128)(2,1)} %get-tuple-element.9.refs_1_, bf16[128,2048]{1,0:T(8,128)(2,1)} %get-tuple-element.10.refs_2_, ...), custom_call_target="tpu_custom_call" | custom-call | tf_op jit(solution)/shard_map/pallas_call | solution.py:489

commit v5 on v4

--- a/solution.py
+++ b/solution.py
@@ -192,6 +192,8 @@
         b = block_at(i, 0)
         da[b] = grad_attn(b)
 
+    da[block_at(0, 2)] = grad_attn(block_at(0, 2))
+
     for i, (src, mid, dst) in enumerate(arrays):
         await_bytes(dst.at[pl.ds(0, 3)], qkv_recv.at[i])
         pltpu.make_async_copy(mid.at[:, :, columns(z)], dst.at[:, z], local_sem.at[i]).wait()
@@ -217,12 +219,12 @@
         head_t = dot(values_t, prob.astype(BF16), NN)
         heads[b] = jnp.where(dead_query, 0.0, head_t).astype(BF16)
 
-    pl.loop(0, NBLK // 2, unroll=2)(forward)
+    pl.loop(0, NBLK // 2, unroll=4)(forward)
     g_wait(0, 3, 1)
     along_x(3, 1)
     g_wait(0, 1, 0)
     along_x(1, 0)
-    pl.loop(NBLK // 2, NBLK, unroll=2)(forward)
+    pl.loop(NBLK // 2, NBLK, unroll=4)(forward)
 
     def backward(slot, b, early=False):
         ids = [lists[0, j, b] for j in range(NB)]
@@ -273,16 +275,12 @@
         g_wait(2, dz, 1)
 
     for dz in (0, 2):
-        @pl.loop(0, 4, step=2)
-        def _(i, dz=dz):
+        for i in range(0, 4, 2):
             for j in range(2):
-                backward(i + j, block_at(i + j, dz), early=dz == 0)
-
-            @pl.when(dz + i > 0)
-            def _():
-                send_dq(block_at(i, dz))
-
-            send_dq(block_at(i + 1, dz))
+                backward(i + j, block_at(i + j, dz), early=dz == 0 or i + j == 0)
+            for j in range(2):
+                if dz + i + j > 0:
+                    send_dq(block_at(i + j, dz))
 
         blocks = [block_at(dx, dz) for dx in range(4)]
         add_parts(blocks)
@@ -335,14 +333,19 @@
     push_dp(whbf.at[rows_at(1 - low, QUART)], wquart, send_sem.at[3], w_recv.at[1], other_low)
 
     add_parts(near + far)
+    dvb[...] = vacc[...].astype(BF16)
+
+    @pl.loop(1, NBLK)
+    def _(o):
+        peer = (me + o) % NBLK
+        push(dvb.at[peer], dv_out.at[:, columns(me)], send_sem.at[1], out_recv.at[2], peer)
+
     dkb[...] = kacc[...].astype(BF16)
-    dvb[...] = vacc[...].astype(BF16)
 
     @pl.loop(1, NBLK)
     def _(o):
         peer = (me + o) % NBLK
         push(dkb.at[peer], dk_out.at[:, columns(me)], send_sem.at[1], out_recv.at[1], peer)
-        push(dvb.at[peer], dv_out.at[:, columns(me)], send_sem.at[1], out_recv.at[2], peer)
 
     back = [
         pltpu.make_async_copy(src.at[me], dst.at[:, columns(me)], local_sem.at[i])

time: 147 us -> 146 us (level)
  no operation moved by 1% of the time
where the time goes in v5:
time: 146 us
  Pallas kernels  145 us (99%)
    pallas_call x1, Pallas kernels, body(): pl.pallas_call(run, out_shape=(rows, rows, rows, rows), in_specs=[hbm, hb...  142 us

profile of v5, /device:TPU:1, one launch (start us, length us, event | category | flops | bytes accessed | tf_op | source)
XLA Modules:
  0.0 145.9 jit_solution(9155102700419133386)
XLA Ops:
  1.3 142.2 %shard_map.102 = (bf16[128,2048]{1,0:T(8,128)(2,1)}, bf16[128,2048]{1,0:T(8,128)(2,1)}, bf16[128,2048]{1,0:T(8,128)(2,1)}, bf16[128,2048]{1,0:T(8,128)(2,1)}) custom-call(bf16[128,2048]{1,0:T(8,128)(2,1)} %refs_0_.1, bf16[128,2048]{1,0:T(8,128)(2,1)} %refs_1_.1, bf16[128,2048]{1,0:T(8,128)(2,1)} %refs_2_.1, bf16[128,2048]{1,0:T(8,128)(2,1)} %refs_3_.1, ...), custom_call_target="tpu_custom_call" | custom-call | flops 4000000000 | bytes 8000000 | tf_op jit(solution)/shard_map/pallas_call | solution.py:430
  143.5 2.4 %shard_map.103 = (bf16[128,2048]{1,0:T(8,128)(2,1)}, bf16[128,2048]{1,0:T(8,128)(2,1)}, bf16[128,2048]{1,0:T(8,128)(2,1)}, bf16[128,2048]{1,0:T(8,128)(2,1)}) custom-call(bf16[128,2048]{1,0:T(8,128)(2,1)} %get-tuple-element.8.refs_0_, bf16[128,2048]{1,0:T(8,128)(2,1)} %get-tuple-element.9.refs_1_, bf16[128,2048]{1,0:T(8,128)(2,1)} %get-tuple-element.10.refs_2_, ...), custom_call_target="tpu_custom_call" | custom-call | tf_op jit(solution)/shard_map/pallas_call | solution.py:492
